TPU v7x, 32 devices: a whole 2x2x4 slice. The times are simulated.
32 devices in a mesh: px: 4 (over x, core), py: 8 (over z, y).
Axes of the slice: x: 2, y: 2, z: 4, core: 2. Of those that a mesh axis runs over, the one named last changes fastest.
Arguments:
- centroids: float32 [3, 524288], P(None, ('px', 'py')), may hold values from 0 to 3
- volumes: float32 [524288], P(('px', 'py')), may hold values from 0.3 to 3
- densities: float32 [524288], P(('px', 'py')), may hold values from 0.01 to 1
- sens_in: float32 [524288], P(('px', 'py')), may hold values from -192 to 192
- local_first: int32 [2048], P(('px', 'py')), may hold values from 0 to 62, as said below
- local_second: int32 [2048], P(('px', 'py')), may hold values from 1 to 63, as said below
- pair_count: int32 [32, 32], P(('px', 'py')), may hold values from 0 to 4, as said below
- pair_mine: int32 [32, 32, 4], P(('px', 'py')), may hold values from 0 to 63, as said below
Outputs:
- filtered: float32 [524288], P(('px', 'py'))
- sensitivity: float32 [524288], P(('px', 'py'))
Inputs may be any that keep to these rules, and one draw needn't show every extreme that they name: `pair_count`: Symmetric, zero on the diagonal, 1 to 4 elsewhere; some partition has 4 pairs with every other one. `pair_mine`: the 4 entries for one d and p are distinct; slot s of (d, p) and slot s of (p, d) name the same pair; slots at or past pair_count[d, p] are unused. local_first < local_second; no pair repeats within a partition. `local_second`: as for local_first.
All inputs are finite; a program needn't handle non-finite values.
Results may differ from a plain program's by a relative error of at most 0.004.
Values may be sent and summed in bfloat16 or wider, within the bound.
No kernel may reach another device: no remote copies, remote signals or barrier semaphores. Data moves between devices by JAX's collectives and lax.ppermute only.
A program may use at most 64 MiB of HBM per device.

v0:
```python
import functools

import jax
import jax.numpy as jnp
from jax import lax
from jax.experimental import pallas as pl
from jax.experimental.pallas import tpu as pltpu
from jax.sharding import PartitionSpec as P

BLK = 256
HALF = BLK // 2
AXES = ("px", "py")
ROWS = 8
WORDS = 5
PEER_ROWS = 24
FEATURES = 32
COORD = 16384.0
VOLUME = 21845.0
DENSITY = 65535.0
MIDDLE = 1.5
TINY = 4e-6
BACK = 16
LOAD = 4
WIDTH = 1
LOOK = 3
DEPTH = 12
KEEP_LIMIT = 20 << 20
MIB = 1 << 20

VMEM = pl.BlockSpec(memory_space=pltpu.VMEM)
SMEM = pl.BlockSpec(memory_space=pltpu.SMEM)
HBM = pl.BlockSpec(memory_space=pltpu.HBM)


def fixed(value, steps):
    return (value * steps + 0.5).astype(jnp.int32)


def two_halves(first, second):
    return first | (second << 16)


def pack_kernel(chosen_in, cent_in, vol_in, dens_in, payload, words, chosen, cent, vol, dens, sems):
    blocks = words.shape[0]
    waits = fetch(
        [(cent_in, cent), (vol_in, vol), (dens_in, dens), (chosen_in, chosen)], sems
    )
    words[...] = jnp.zeros_like(words)
    for wait in waits:
        wait()
    for b in range(blocks):
        low = cent[:, b * BLK : b * BLK + HALF]
        high = cent[:, b * BLK + HALF : (b + 1) * BLK]
        words[b, 0:3, :] = two_halves(fixed(low, COORD), fixed(high, COORD))
    for row, source, steps in ((3, vol, VOLUME), (4, dens, DENSITY)):
        low = source[pl.ds(0, blocks, stride=2), :]
        high = source[pl.ds(1, blocks, stride=2), :]
        words[:, row, :] = two_halves(fixed(low, steps), fixed(high, steps))
    slots, peers = chosen.shape

    def send(p, carry):
        for s in range(slots):
            payload[p, WORDS * s : WORDS * (s + 1), :] = words[chosen[s, p], 0:WORDS, :]
        return carry

    lax.fori_loop(0, peers, send, 0, unroll=4)


def decode(word):
    row = lax.broadcasted_iota(jnp.int32, (ROWS, BLK), 0)
    step = jnp.where(
        row < 3,
        1.0 / COORD,
        jnp.where(row == 3, 1.0 / VOLUME, jnp.where(row == 4, 1.0 / DENSITY, 0.0)),
    )
    parts = jnp.concatenate([word & 0xFFFF, lax.shift_right_logical(word, 16)], axis=1)
    held = parts.astype(jnp.float32) * step
    volume = held[3:4, :]
    values = jnp.where(row == 4, held * volume, held).astype(jnp.bfloat16)
    place = jnp.where(row < 3, held - MIDDLE, 0.0)
    high = place.astype(jnp.bfloat16).astype(jnp.float32)
    low = place - high
    norm = jnp.sum(place * place, axis=0, keepdims=True)
    norm1 = norm.astype(jnp.bfloat16).astype(jnp.float32)
    rest = norm - norm1
    norm2 = rest.astype(jnp.bfloat16).astype(jnp.float32)
    norm3 = rest - norm2
    one = jnp.where(row == 6, 1.0, 0.0)
    far1 = high + jnp.where(
        row == 3, norm1, jnp.where(row == 4, norm2, jnp.where(row == 5, norm3, one))
    )
    far2 = low + jnp.where((row == 3) | (row == 4), 1.0, 0.0)
    far = jnp.concatenate([far1, far2], axis=0).astype(jnp.bfloat16)
    far = jnp.concatenate([far, far], axis=0)
    near1 = -2.0 * high + jnp.where(
        (row >= 3) & (row <= 5), 1.0, jnp.where(row == 6, norm1, 0.0)
    )
    near2 = -2.0 * high + jnp.where(row == 3, norm2, jnp.where(row == 4, norm3, 0.0))
    near34 = -2.0 * low
    near = jnp.concatenate([near1, near2, near34, near34], axis=0).astype(jnp.bfloat16)
    return far, near, values


def product(rows, tile):
    return jnp.dot(rows, tile, preferred_element_type=jnp.float32)


def product_t(rows, tile):
    return lax.dot_general(
        rows, tile, (((1,), (1,)), ((), ())), preferred_element_type=jnp.float32
    )


def cone(squares, u):
    root = squares[u] * lax.rsqrt(jnp.maximum(squares[u], TINY))
    return jnp.maximum((1.0 - root).astype(jnp.bfloat16), 0)


def staged(groups, peel, width, tiles, kept, sems, squares, results, square, use, settle, beside=None):
    def place(d, u):
        return d % DEPTH * width + u

    def copy(k, count):
        part = pl.ds(k * DEPTH * width, count * width)
        return pltpu.make_async_copy(tiles.at[part], kept.at[part], sems.at[k])

    slots = LOOK + 1

    def distances(g, d):
        for u in range(width):
            squares[(d % slots) * width + u] = square(g * width + u, place(d, u))

    def cones(view, d):
        for u in range(width):
            view[d * width + u] = cone(squares, (d % slots) * width + u)

    def sums(view, g, d):
        for u in range(width):
            parts = use(g * width + u, place(d, u), view[d * width + u])
            for result, part in zip(results, parts):
                result[d * width + u] = part

    def settled(g, count):
        for d in range(count):
            for u in range(width):
                settle((g + d) * width + u, d * width + u)

    def view_from(g, count):
        return tiles.at[pl.ds(g * width, count * width)]

    for d in range(slots):
        distances(d, d)
    cones(view_from(0, 1), 0)
    turns = (groups - slots - peel) // DEPTH

    def steps(g, count):
        view = view_from(g, count + 1)
        for d in range(count):
            sums(view, g + d, d)
            distances(g + d + slots, d + slots)
            cones(view, d + 1)
        settled(g, count)

    def turn(k, carry):
        if beside is not None:
            beside(k)
        steps(k * DEPTH, DEPTH)
        if kept is not None:
            copy(k, DEPTH).start()
        return carry

    lax.fori_loop(0, turns, turn, 0)
    g = turns * DEPTH
    last = peel + slots
    view = view_from(g, last)
    for d in range(last):
        sums(view, g + d, d)
        if d < peel:
            distances(g + d + slots, d + slots)
        if d + 1 < last:
            cones(view, d + 1)
    if kept is not None:
        copy(turns, last).start()
    settled(g, last)

    def wait():
        def one(k, carry):
            copy(k, DEPTH).wait()
            return carry

        lax.fori_loop(0, turns, one, 0)
        copy(turns, last).wait()

    return wait


def peeled(most):
    return (most - LOOK - 1) % DEPTH


def padded(groups, peel):
    least = LOOK + 1 + peel
    return jnp.maximum((groups - least + DEPTH - 1) // DEPTH, 0) * DEPTH + least


def chunked(size, room, width, ring, squares, results, square, use, settle):
    def chunk(c, carry):
        base = c * room
        left = jnp.minimum(size - base, room)
        staged(
            padded((left + width - 1) // width, 0),
            0,
            width,
            ring,
            None,
            None,
            squares,
            results,
            lambda i, at: square(base + i, at),
            lambda i, at, tile: use(base + i, at, tile),
            lambda i, at: settle(jnp.where(i < left, base + i, size), at),
        )
        return carry

    lax.fori_loop(0, jnp.maximum((size + room - 1) // room, 1), chunk, 0)


def fetch(pairs, sems):
    copies = [pltpu.make_async_copy(a, b, sems.at[k]) for k, (a, b) in enumerate(pairs)]
    for copy in copies:
        copy.start()
    return [copy.wait for copy in copies]


def local_kernel(
    width, first_in, second_in, counts_in, chosen_in, words, total, kept, near, plan,
    first, second, counts, chosen, ring, far_t, vals, squares, sums0, sums1, sems, self_sems, pair_sems,
):
    blocks = words.shape[0]
    pairs = first.shape[0]
    peers = counts.shape[1]
    slots = chosen.shape[0]
    waits = fetch(
        [(first_in, first), (second_in, second), (counts_in, counts), (chosen_in, chosen)], sems
    )

    def square_self(b, at):
        f, n, v = decode(words[b])
        f = f.T
        far_t[b] = f
        near[b] = n
        vals[b] = v
        return product(f, n)

    def use_self(b, at, tile):
        return (product(vals[b], tile),)

    def settle_self(b, at):
        total[b] = sums0[at]

    part = pl.ds(0, blocks)
    wait_self = staged(
        blocks // width, peeled(blocks // width), width, ring.at[part], kept.at[part], self_sems, squares, (sums0,),
        square_self, use_self, settle_self,
    )
    for wait in waits:
        wait()

    def square_pair(j, at):
        return product(far_t[second[j]], near[first[j]])

    def use_pair(j, at, tile):
        return product(vals[second[j]], tile), product_t(vals[first[j]], tile)

    def settle_pair(j, at):
        total[first[j]] += sums0[at]
        total[second[j]] += sums1[at]

    length = plan_length(plan)
    turns = (pairs // width - LOOK - 1) // DEPTH
    share = -(-peers // turns)
    plan[0] = 0

    def collect(k):
        found = plan[0]
        for q in range(share):
            p = k * share + q
            peer = jnp.minimum(p, peers - 1)
            count = jnp.where(p < peers, counts[0, peer], 0)
            for s in range(slots):
                plan[1 + found] = peer * slots + s
                plan[1 + length + found] = chosen[s, peer]
                found = found + (s < count).astype(jnp.int32)
        plan[0] = found

    part = pl.ds(blocks, pairs)
    wait_pair = staged(
        pairs // width, peeled(pairs // width), width, ring.at[part], kept.at[part], pair_sems, squares, (sums0, sums1),
        square_pair, use_pair, settle_pair, collect,
    )

    for i in range(2 * DEPTH * width):
        plan[1 + plan[0] + i] = 0
        plan[1 + length + plan[0] + i] = 0
    wait_self()
    wait_pair()


def plan_length(plan):
    return (plan.shape[0] - 1) // 2


def far_word(received, slots, place):
    peer, slot = place // slots, place % slots
    return received[pl.ds(peer * PEER_ROWS + slot * WORDS, ROWS), :]


def cross_kernel(
    width, keep, plan, chosen_in, received, near, total_in, sens_in, filtered, ratio, payload, *rest
):
    kept = None
    if keep:
        kept, *rest = rest
    ring, total, flat, vals, sens, chosen, squares, sums0, sems, *ring_sems = rest
    blocks = near.shape[0]
    waits = fetch([(chosen_in, chosen), (sens_in, sens)], sems)
    total[...] = total_in[...]
    slots, peers = chosen.shape
    size, length = plan[0], plan_length(plan)

    def square(i, at):
        f, unused, v = decode(far_word(received, slots, plan[1 + i]))
        vals[at] = v
        return product(f.T, near[plan[1 + length + i]])

    def use(i, at, tile):
        return (product(vals[at], tile),)

    def settle(i, at):
        total[plan[1 + length + i]] += jnp.where(i < size, sums0[at], 0.0)

    if keep:
        peel = peeled((peers - 1) * slots // width)
        groups = padded((size + width - 1) // width, peel)
        wait_tiles = staged(
            groups, peel, width, ring, kept, ring_sems[0], squares, (sums0,), square, use, settle
        )
    else:
        room = ring.shape[0] - (DEPTH + LOOK + 1) * width
        chunked(size, room, width, ring, squares, (sums0,), square, use, settle)
    for wait in waits:
        wait()
    base = total[:, 3, :]
    filt = total[:, 4, :] / base
    for half in range(2):
        rows = pl.ds(half, blocks, stride=2)
        lanes = slice(half * HALF, (half + 1) * HALF)
        filtered[rows, :] = filt[:, lanes]
        part = sens[rows, :] / base[:, lanes]
        flat[rows, :] = part.astype(jnp.bfloat16).astype(jnp.float32)
    ratio[...] = jnp.zeros_like(ratio)
    for half in range(2):
        lanes = slice(half * HALF, (half + 1) * HALF)
        ratio[:, 0, lanes] = flat[pl.ds(half, blocks, stride=2), :]

    def send(p, carry):
        for s in range(slots):
            payload[p, 2 * s : 2 * s + 2, :] = flat[pl.ds(2 * chosen[s, p], 2), :]
        return carry

    lax.fori_loop(0, peers, send, 0, unroll=4)
    if keep:
        wait_tiles()


def tile_loads(width, kept, tiles, sems):
    each = width // LOAD

    def copy(k):
        part = pl.ds(k * LOAD, LOAD)
        return pltpu.make_async_copy(kept.at[part], tiles.at[part], sems.at[k])

    def start(a, b):
        def one(k, carry):
            copy(k).start()
            return carry

        lax.fori_loop(a * each, b * each, one, 0)

    def ready(k):
        for j in range(each):
            copy(k * each + j).wait()

    return start, ready


def back_local_kernel(
    width, first_in, second_in, ratio, kept, total, first, second, tiles, sems, tile_sems
):
    blocks = ratio.shape[0]
    pairs = first.shape[0]
    start, ready = tile_loads(width, kept, tiles, tile_sems)
    waits = fetch([(first_in, first), (second_in, second)], sems)
    start(blocks // width, (blocks + pairs) // width)
    start(0, blocks // width)
    total[...] = jnp.zeros_like(total)

    def rows(b):
        return ratio[b].astype(jnp.bfloat16)

    for wait in waits:
        wait()

    def pair(k, carry):
        ready(blocks // width + k)
        ids = [(first[k * width + u], second[k * width + u]) for u in range(width)]
        sums = []
        for u, (a, b) in enumerate(ids):
            tile = tiles[blocks + k * width + u]
            sums.append((product(rows(b), tile), product_t(rows(a), tile)))
        for (a, b), (to_first, to_second) in zip(ids, sums):
            total[a] += to_first
            total[b] += to_second
        return carry

    lax.fori_loop(0, pairs // width, pair, 0)

    def own(k, carry):
        ready(k)
        sums = [product(rows(k * width + u), tiles[k * width + u]) for u in range(width)]
        for u in range(width):
            total[k * width + u] += sums[u]
        return carry

    lax.fori_loop(0, blocks // width, own, 0)


def far_ratio(ratio, place):
    row0 = ratio[pl.ds(place * 2, 1), :]
    row1 = ratio[pl.ds(place * 2 + 1, 1), :]
    return jnp.concatenate([row0, row1], axis=1).astype(jnp.bfloat16)


def finish_back(blocks, vol, total, out):
    for half in range(2):
        rows = pl.ds(half, blocks, stride=2)
        lanes = slice(half * HALF, (half + 1) * HALF)
        out[rows, :] = vol[rows, :] * total[:, 0, lanes]


def back_cross_kernel(
    width, least, plan_in, ratio, kept, total_in, vol_in, out,
    total, vol, tiles, plan, sems, tile_sems,
):
    blocks = total.shape[0]
    start, ready = tile_loads(width, kept, tiles, tile_sems)
    wait_plan, *waits = fetch([(plan_in, plan), (vol_in, vol)], sems)
    early = -(-least // width)
    start(0, early)
    total[...] = total_in[...]
    wait_plan()
    size, length = plan[0], plan_length(plan)
    groups = (size + width - 1) // width
    start(early, groups)

    def turn(k, carry):
        ready(k)
        sums = []
        for u in range(width):
            i = k * width + u
            part = product(far_ratio(ratio, plan[1 + i]), tiles[i])
            part = jnp.where(i < size, part, 0.0)
            sums.append((plan[1 + length + i], part))
        for b, part in sums:
            total[b, 0:1, :] += part
        return carry

    lax.fori_loop(0, groups, turn, 0)
    for wait in waits:
        wait()
    finish_back(blocks, vol, total, out)


def back_again_kernel(
    width, slots, plan, ratio, received, near, total_in, vol_in, out,
    total, vol, ring, squares, sums0, sems,
):
    blocks = total.shape[0]
    waits = fetch([(vol_in, vol)], sems)
    total[...] = total_in[...]
    size, length = plan[0], plan_length(plan)

    def square(i, at):
        f, unused, v = decode(far_word(received, slots, plan[1 + i]))
        return product(f.T, near[plan[1 + length + i]])

    def use(i, at, tile):
        return (product(far_ratio(ratio, plan[1 + i]), tile),)

    def settle(i, at):
        total[plan[1 + length + i], 0:1, :] += jnp.where(i < size, sums0[at], 0.0)

    room = ring.shape[0] - (DEPTH + LOOK + 1) * width
    chunked(size, room, width, ring, squares, (sums0,), square, use, settle)
    for wait in waits:
        wait()
    finish_back(blocks, vol, total, out)


def in_hbm(array):
    return pltpu.with_memory_space_constraint(array, pltpu.HBM)


def params(mib):
    return pltpu.CompilerParams(vmem_limit_bytes=mib * MIB)


def shards(
    centroids, volumes, densities, sens_in, local_first, local_second, pair_count, pair_mine
):
    elements = volumes.shape[0]
    blocks = elements // BLK
    flat_rows = elements // HALF
    vol = in_hbm(volumes.reshape(flat_rows, HALF))
    dens = in_hbm(densities.reshape(flat_rows, HALF))
    sens = in_hbm(sens_in.reshape(flat_rows, HALF))
    local_first, local_second = in_hbm(local_first), in_hbm(local_second)
    chosen = in_hbm(pair_mine[0].T)
    slots, peers = chosen.shape
    places = peers * slots
    pairs = local_first.shape[0]
    longest = 2 * places
    f32, bf16, i32 = jnp.float32, jnp.bfloat16, jnp.int32
    shape = jax.ShapeDtypeStruct
    width = WIDTH
    flat = pltpu.VMEM((flat_rows, HALF), f32)
    sums = pltpu.VMEM((blocks, ROWS, BLK), f32)
    square = pltpu.VMEM(((LOOK + 1) * width, BLK, BLK), f32)
    tile_bytes = BLK * BLK * 2
    keep = places * tile_bytes <= KEEP_LIMIT
    most = (places - slots) // width
    turns = most // DEPTH
    held = max(most * width, -(-most * width // BACK) * BACK)
    ring = pltpu.VMEM((held if keep else KEEP_LIMIT // tile_bytes, BLK, BLK), bf16)
    steps = DEPTH + LOOK + 1
    results = pltpu.VMEM((steps * width, ROWS, BLK), f32)
    ring_sems = pltpu.SemaphoreType.DMA((turns + 1,))
    table = pltpu.SMEM(chosen.shape, i32)
    row = pltpu.SMEM((pairs,), i32)

    payload, words = pl.pallas_call(
        pack_kernel,
        out_shape=(shape((peers, PEER_ROWS, HALF), i32), shape((blocks, ROWS, HALF), i32)),
        in_specs=[HBM] * 4,
        out_specs=(VMEM, VMEM),
        scratch_shapes=[
            table,
            pltpu.VMEM(centroids.shape, f32),
            flat,
            flat,
            pltpu.SemaphoreType.DMA((4,)),
        ],
        compiler_params=params(8),
        name="pack",
    )(chosen, in_hbm(centroids), vol, dens)
    received = lax.all_to_all(payload, AXES, split_axis=0, concat_axis=0, tiled=True)
    total, tiles, near, plan = pl.pallas_call(
        functools.partial(local_kernel, width),
        out_shape=(
            shape((blocks, ROWS, BLK), f32),
            pltpu.HBM((blocks + pairs, BLK, BLK), bf16),
            shape((blocks, FEATURES, BLK), bf16),
            shape((1 + 2 * longest,), i32),
        ),
        in_specs=[HBM, HBM, HBM, HBM, VMEM],
        out_specs=(VMEM, HBM, VMEM, SMEM),
        scratch_shapes=[
            row,
            row,
            pltpu.SMEM(pair_count.shape, i32),
            table,
            pltpu.VMEM((blocks + pairs, BLK, BLK), bf16),
            pltpu.VMEM((blocks, BLK, FEATURES), bf16),
            pltpu.VMEM((blocks, ROWS, BLK), bf16),
            square,
            results,
            results,
            pltpu.SemaphoreType.DMA((4,)),
            pltpu.SemaphoreType.DMA((blocks // width // DEPTH + 1,)),
            pltpu.SemaphoreType.DMA((pairs // width // DEPTH + 1,)),
        ],
        compiler_params=params(48),
        cost_estimate=pl.CostEstimate(
            flops=(blocks + pairs) * BLK * BLK * 100, bytes_accessed=1 << 20, transcendentals=0
        ),
        name="local",
    )(local_first, local_second, in_hbm(pair_count), chosen, words)
    received = received.reshape(peers * PEER_ROWS, HALF)
    filtered, ratio, payload2, *cross_tiles = pl.pallas_call(
        functools.partial(cross_kernel, width, keep),
        out_shape=(
            shape((flat_rows, HALF), f32),
            shape((blocks, ROWS, BLK), f32),
            shape((peers, 2 * slots, HALF), f32),
        )
        + ((pltpu.HBM((held, BLK, BLK), bf16),) if keep else ()),
        in_specs=[SMEM, HBM, VMEM, VMEM, VMEM, HBM],
        out_specs=(VMEM, VMEM, VMEM) + ((HBM,) if keep else ()),
        scratch_shapes=[
            ring,
            sums,
            flat,
            pltpu.VMEM((steps * width, ROWS, BLK), bf16),
            flat,
            table,
            square,
            results,
            pltpu.SemaphoreType.DMA((2,)),
        ]
        + ([ring_sems] if keep else []),
        compiler_params=params(48),
        name="cross",
    )(plan, chosen, received, near, total, sens)
    received2 = lax.all_to_all(payload2, AXES, split_axis=0, concat_axis=0, tiled=True)
    back = pl.pallas_call(
        functools.partial(back_local_kernel, BACK),
        out_shape=shape((blocks, ROWS, BLK), f32),
        in_specs=[HBM, HBM, VMEM, HBM],
        out_specs=VMEM,
        scratch_shapes=[
            row,
            row,
            pltpu.VMEM((blocks + pairs, BLK, BLK), bf16),
            pltpu.SemaphoreType.DMA((2,)),
            pltpu.SemaphoreType.DMA(((blocks + pairs) // LOAD,)),
        ],
        compiler_params=params(48),
        cost_estimate=pl.CostEstimate(
            flops=(blocks + pairs) * BLK * BLK * 100, bytes_accessed=1 << 20, transcendentals=0
        ),
        name="back_local",
    )(local_first, local_second, ratio, in_hbm(tiles))
    received2 = received2.reshape(places * 2, HALF)
    common = [sums, flat, pltpu.VMEM((places, BLK, BLK), bf16) if keep else ring]
    if keep:
        kernel, operands, specs = back_cross_kernel, (in_hbm(cross_tiles[0]),), [HBM]
        kernel = functools.partial(kernel, BACK, peers - 1)
        scratch = [pltpu.SMEM((1 + 2 * longest,), i32), pltpu.SemaphoreType.DMA((2,)), pltpu.SemaphoreType.DMA((places // LOAD,))]
    else:
        kernel, operands, specs = back_again_kernel, (received, near), [VMEM, VMEM]
        scratch = [square, pltpu.VMEM((steps * width, 1, BLK), f32), pltpu.SemaphoreType.DMA((1,))]
        kernel = functools.partial(kernel, width, slots)
    sensitivity = pl.pallas_call(
        kernel,
        out_shape=shape((flat_rows, HALF), f32),
        in_specs=[pl.BlockSpec(memory_space=pl.ANY) if keep else SMEM, VMEM, *specs, VMEM, HBM],
        out_specs=VMEM,
        scratch_shapes=common + scratch,
        compiler_params=params(48),
        name="back_cross",
    )(plan, received2, *operands, back, vol)
    return (filtered.reshape(-1), sensitivity.reshape(-1))


def solution(mesh):
    return jax.shard_map(
        shards,
        mesh=mesh,
        in_specs=(
            P(None, AXES),
            P(AXES),
            P(AXES),
            P(AXES),
            P(AXES),
            P(AXES),
            P(AXES, None),
            P(AXES, None, None),
        ),
        out_specs=(P(AXES), P(AXES)),
        check_vma=False,
    )
```

profile of v0, /device:TPU:0, one launch (start us, length us, event | category | flops | bytes accessed | tf_op | source)
XLA Modules:
  0.0 53.9 jit_solution(14733273469211257676)
XLA Ops:
  0.6 2.1 %pack.1 = (s32[32,24,128]{2,1,0:T(8,128)}, s32[64,8,128]{2,1,0:T(8,128)S(1)}) custom-call(s32[4,32]{1,0:T(4,128)} %bitcast.17, f32[3,16384]{1,0:T(4,128)} %cent_in.1, f32[128,128]{1,0:T(8,128)} %bitcast.12, f32[128,128]{1,0:T(8,128)} %bitcast.16), custom_call_target="tpu_custom_call" | custom-call | tf_op jit(solution)/shard_map/pack/pallas_call | solution.py:551
  2.8 7.3 %all-to-all-start = ((s32[32,24,128]{2,1,0:T(8,128)}), s32[32,24,128]{2,1,0:T(8,128)S(1)}, u32[]{:S(2)}, u32[]{:S(2)}) async-start(s32[32,24,128]{2,1,0:T(8,128)} %get-tuple-element.14), calls=%async_computation | async-start | bytes 786432 | tf_op jit(solution)/shard_map/all_to_all | solution.py:566
  10.1 12.9 %local.1 = (f32[64,8,256]{2,1,0:T(8,128)S(1)}, bf16[128,256,256]{2,1,0:T(8,128)(2,1)}, bf16[64,32,256]{2,1,0:T(8,128)(2,1)S(1)}, s32[513]{0:T(1024)S(1)}) custom-call(s32[64]{0:T(128)} %first_in.3, s32[64]{0:T(128)} %second_in.3, s32[1,32]{1,0:T(1,128)} %counts_in.1, s32[4,32]{1,0:T(4,128)} %bitcast.18, s32[64,8,128]{2,1,0:T(8,128)S(1)} %get-tuple-element.12.words), custom_call_target="tpu_custom_call" | custom-call | flops 838860800 | bytes 1048576 | tf_op jit(solution)/shard_map/local/pallas_call | solution.py:567
  23.0 0.6 %all-to-all-done = s32[32,24,128]{2,1,0:T(8,128)S(1)} async-done(((s32[32,24,128]{2,1,0:T(8,128)}), s32[32,24,128]{2,1,0:T(8,128)S(1)}, u32[]{:S(2)}, u32[]{:S(2)}) %all-to-all-start) | async-done | bytes 393248 | tf_op jit(solution)/shard_map/all_to_all | solution.py:566
  23.6 11.1 %cross.1 = (f32[128,128]{1,0:T(8,128)}, f32[64,8,256]{2,1,0:T(8,128)S(1)}, f32[32,8,128]{2,1,0:T(8,128)}, bf16[128,256,256]{2,1,0:T(8,128)(2,1)}) custom-call(s32[513]{0:T(1024)S(1)} %get-tuple-element.13.plan.plan_in, s32[4,32]{1,0:T(4,128)} %bitcast.19, s32[768,128]{1,0:T(8,128)S(1)} %bitcast.10, bf16[64,32,256]{2,1,0:T(8,128)(2,1)S(1)} %get-tuple-element.15.near, ...), custom_call_target="tpu_custom_call" | custom-call | tf_op jit(solution)/shard_map/cross/pallas_call | solution.py:599
  34.7 5.3 %all-to-all-start.1 = ((f32[32,8,128]{2,1,0:T(8,128)}), f32[32,8,128]{2,1,0:T(8,128)S(1)}, u32[]{:S(2)}, u32[]{:S(2)}) async-start(f32[32,8,128]{2,1,0:T(8,128)} %get-tuple-element.18), calls=%async_computation.1 | async-start | bytes 262144 | tf_op jit(solution)/shard_map/all_to_all | solution.py:624
  40.1 7.3 %back_local.1.total_in = f32[64,8,256]{2,1,0:T(8,128)S(1)} custom-call(s32[64]{0:T(128)} %first_in.3, s32[64]{0:T(128)} %second_in.3, f32[64,8,256]{2,1,0:T(8,128)S(1)} %get-tuple-element.20.ratio, bf16[128,256,256]{2,1,0:T(8,128)(2,1)} %get-tuple-element.21.kept), custom_call_target="tpu_custom_call" | custom-call | flops 838860800 | bytes 1048576 | tf_op jit(solution)/shard_map/back_local/pallas_call | solution.py:625
  47.3 0.5 all-to-all-done.1
  47.8 6.1 %back_cross.1 = f32[128,128]{1,0:T(8,128)} custom-call(s32[513]{0:T(1024)S(1)} %get-tuple-element.13.plan.plan_in, f32[256,128]{1,0:T(8,128)S(1)} %bitcast.11, bf16[128,256,256]{2,1,0:T(8,128)(2,1)} %get-tuple-element.19.kept, f32[64,8,256]{2,1,0:T(8,128)S(1)} %back_local.1.total_in, f32[128,128]{1,0:T(8,128)} %bitcast.13), custom_call_target="tpu_custom_call" | custom-call | tf_op jit(solution)/shard_map/back_cross/pallas_call | solution.py:653
Async XLA Ops:
  2.8 20.9 %all-to-all-start = ((s32[32,24,128]{2,1,0:T(8,128)}), s32[32,24,128]{2,1,0:T(8,128)S(1)}, u32[]{:S(2)}, u32[]{:S(2)}) async-start(s32[32,24,128]{2,1,0:T(8,128)} %get-tuple-element.14), calls=%async_computation | async-start | bytes 786432 | tf_op jit(solution)/shard_map/all_to_all | solution.py:566
  34.7 13.1 %all-to-all-start.1 = ((f32[32,8,128]{2,1,0:T(8,128)}), f32[32,8,128]{2,1,0:T(8,128)S(1)}, u32[]{:S(2)}, u32[]{:S(2)}) async-start(f32[32,8,128]{2,1,0:T(8,128)} %get-tuple-element.18), calls=%async_computation.1 | async-start | bytes 262144 | tf_op jit(solution)/shard_map/all_to_all | solution.py:624
where the time goes:
time: 53.5 us; the launch traced here: 53.9 us
  Pallas kernels  39.5 us (74%)
  starting transfers between devices  12.6 us (24%)
  waiting for transfers between devices  1.09 us (2%)
  between operations  0.68 us (1%)
    pallas_call x1, Pallas kernels, shards(): pl.pallas_call(functools.partial(local_kernel, width), out_shape=(shape((...  12.9 us
    pallas_call x1, Pallas kernels, shards(): pl.pallas_call(functools.partial(cross_kernel, width, keep), out_shape=(s...  11.1 us
    all_to_all x1, starting transfers between devices, shards(): lax.all_to_all(payload, AXES, split_axis=0, concat_axis=0, tiled=True)  7.3 us
    pallas_call x1, Pallas kernels, shards(): pl.pallas_call(functools.partial(back_local_kernel, BACK), out_shape=shap...  7.26 us
    pallas_call x1, Pallas kernels, shards(): pl.pallas_call(kernel, out_shape=shape((flat_rows, HALF), f32), in_specs=...  6.13 us
    all_to_all x1, starting transfers between devices, shards(): lax.all_to_all(payload2, AXES, split_axis=0, concat_axis=0, tiled=True)  5.33 us
    pallas_call x1, Pallas kernels, shards(): pl.pallas_call(pack_kernel, out_shape=(shape((peers, PEER_ROWS, HALF), i3...  2.13 us
  transfers between devices with their start and end apart: 2, of which 2 were waited for; matrix products, arithmetic and copies ran while one was open for 0% of the time, Pallas kernels for 37%

commit v1 on v0

--- a/solution.py
+++ b/solution.py
@@ -19,11 +19,12 @@
 DENSITY = 65535.0
 MIDDLE = 1.5
 TINY = 4e-6
+STAY = 8
 BACK = 16
 LOAD = 4
 WIDTH = 1
 LOOK = 3
-DEPTH = 12
+DEPTH = 20
 KEEP_LIMIT = 20 << 20
 MIB = 1 << 20
 
@@ -320,8 +321,8 @@
 ):
     kept = None
     if keep:
-        kept, *rest = rest
-    ring, total, flat, vals, sens, chosen, squares, sums0, sems, *ring_sems = rest
+        kept, stay, *rest = rest
+    ring, total, vals, sens, chosen, squares, sums0, sems, *ring_sems = rest
     blocks = near.shape[0]
     waits = fetch([(chosen_in, chosen), (sens_in, sens)], sems)
     total[...] = total_in[...]
@@ -348,6 +349,8 @@
     else:
         room = ring.shape[0] - (DEPTH + LOOK + 1) * width
         chunked(size, room, width, ring, squares, (sums0,), square, use, settle)
+    if keep:
+        waits += fetch([(ring.at[pl.ds(0, stay.shape[0])], stay)], ring_sems[1])
     for wait in waits:
         wait()
     base = total[:, 3, :]
@@ -357,15 +360,10 @@
         lanes = slice(half * HALF, (half + 1) * HALF)
         filtered[rows, :] = filt[:, lanes]
         part = sens[rows, :] / base[:, lanes]
-        flat[rows, :] = part.astype(jnp.bfloat16).astype(jnp.float32)
-    ratio[...] = jnp.zeros_like(ratio)
-    for half in range(2):
-        lanes = slice(half * HALF, (half + 1) * HALF)
-        ratio[:, 0, lanes] = flat[pl.ds(half, blocks, stride=2), :]
-
+        ratio[rows, :] = part.astype(jnp.bfloat16).astype(jnp.float32)
     def send(p, carry):
         for s in range(slots):
-            payload[p, 2 * s : 2 * s + 2, :] = flat[pl.ds(2 * chosen[s, p], 2), :]
+            payload[p, 2 * s : 2 * s + 2, :] = ratio[pl.ds(2 * chosen[s, p], 2), :]
         return carry
 
     lax.fori_loop(0, peers, send, 0, unroll=4)
@@ -385,10 +383,10 @@
             copy(k).start()
             return carry
 
-        lax.fori_loop(a * each, b * each, one, 0)
-
-    def ready(k):
-        for j in range(each):
+        lax.fori_loop(a // LOAD, b // LOAD, one, 0)
+
+    def ready(k, u=0):
+        for j in range(u // LOAD, each):
             copy(k * each + j).wait()
 
     return start, ready
@@ -397,16 +395,16 @@
 def back_local_kernel(
     width, first_in, second_in, ratio, kept, total, first, second, tiles, sems, tile_sems
 ):
-    blocks = ratio.shape[0]
+    blocks = total.shape[0]
     pairs = first.shape[0]
     start, ready = tile_loads(width, kept, tiles, tile_sems)
     waits = fetch([(first_in, first), (second_in, second)], sems)
-    start(blocks // width, (blocks + pairs) // width)
-    start(0, blocks // width)
+    start(blocks, blocks + pairs)
+    start(0, blocks)
     total[...] = jnp.zeros_like(total)
 
     def rows(b):
-        return ratio[b].astype(jnp.bfloat16)
+        return far_ratio(ratio, b)
 
     for wait in waits:
         wait()
@@ -419,8 +417,8 @@
             tile = tiles[blocks + k * width + u]
             sums.append((product(rows(b), tile), product_t(rows(a), tile)))
         for (a, b), (to_first, to_second) in zip(ids, sums):
-            total[a] += to_first
-            total[b] += to_second
+            total[a, 0:1, :] += to_first
+            total[b, 0:1, :] += to_second
         return carry
 
     lax.fori_loop(0, pairs // width, pair, 0)
@@ -429,7 +427,7 @@
         ready(k)
         sums = [product(rows(k * width + u), tiles[k * width + u]) for u in range(width)]
         for u in range(width):
-            total[k * width + u] += sums[u]
+            total[k * width + u, 0:1, :] += sums[u]
         return carry
 
     lax.fori_loop(0, blocks // width, own, 0)
@@ -449,33 +447,39 @@
 
 
 def back_cross_kernel(
-    width, least, plan_in, ratio, kept, total_in, vol_in, out,
+    width, least, plan_in, ratio, kept, stay, total_in, vol_in, out,
     total, vol, tiles, plan, sems, tile_sems,
 ):
     blocks = total.shape[0]
     start, ready = tile_loads(width, kept, tiles, tile_sems)
     wait_plan, *waits = fetch([(plan_in, plan), (vol_in, vol)], sems)
-    early = -(-least // width)
-    start(0, early)
+    early = -(-least // width) * width
+    staying = stay.shape[0]
+    start(staying, early)
     total[...] = total_in[...]
     wait_plan()
     size, length = plan[0], plan_length(plan)
     groups = (size + width - 1) // width
-    start(early, groups)
-
-    def turn(k, carry):
-        ready(k)
+    start(early, groups * width)
+
+    def group(k, tile):
         sums = []
         for u in range(width):
             i = k * width + u
-            part = product(far_ratio(ratio, plan[1 + i]), tiles[i])
+            part = product(far_ratio(ratio, plan[1 + i]), tile(u, i))
             part = jnp.where(i < size, part, 0.0)
             sums.append((plan[1 + length + i], part))
         for b, part in sums:
             total[b, 0:1, :] += part
+
+    def turn(k, carry):
+        ready(k)
+        group(k, lambda u, i: tiles[i])
         return carry
 
-    lax.fori_loop(0, groups, turn, 0)
+    ready(0, staying)
+    group(0, lambda u, i: stay[i] if u < staying else tiles[i])
+    lax.fori_loop(1, groups, turn, 0)
     for wait in waits:
         wait()
     finish_back(blocks, vol, total, out)
@@ -505,6 +509,10 @@
     for wait in waits:
         wait()
     finish_back(blocks, vol, total, out)
+
+
+def in_vmem(array):
+    return pltpu.with_memory_space_constraint(array, pltpu.VMEM)
 
 
 def in_hbm(array):
@@ -600,16 +608,15 @@
         functools.partial(cross_kernel, width, keep),
         out_shape=(
             shape((flat_rows, HALF), f32),
-            shape((blocks, ROWS, BLK), f32),
+            shape((flat_rows, HALF), f32),
             shape((peers, 2 * slots, HALF), f32),
         )
-        + ((pltpu.HBM((held, BLK, BLK), bf16),) if keep else ()),
+        + ((pltpu.HBM((held, BLK, BLK), bf16), pltpu.VMEM((STAY, BLK, BLK), bf16)) if keep else ()),
         in_specs=[SMEM, HBM, VMEM, VMEM, VMEM, HBM],
-        out_specs=(VMEM, VMEM, VMEM) + ((HBM,) if keep else ()),
+        out_specs=(VMEM, VMEM, VMEM) + ((HBM, VMEM) if keep else ()),
         scratch_shapes=[
             ring,
             sums,
-            flat,
             pltpu.VMEM((steps * width, ROWS, BLK), bf16),
             flat,
             table,
@@ -617,7 +624,7 @@
             results,
             pltpu.SemaphoreType.DMA((2,)),
         ]
-        + ([ring_sems] if keep else []),
+        + ([ring_sems, pltpu.SemaphoreType.DMA((1,))] if keep else []),
         compiler_params=params(48),
         name="cross",
     )(plan, chosen, received, near, total, sens)
@@ -643,7 +650,7 @@
     received2 = received2.reshape(places * 2, HALF)
     common = [sums, flat, pltpu.VMEM((places, BLK, BLK), bf16) if keep else ring]
     if keep:
-        kernel, operands, specs = back_cross_kernel, (in_hbm(cross_tiles[0]),), [HBM]
+        kernel, operands, specs = back_cross_kernel, (in_hbm(cross_tiles[0]), in_vmem(cross_tiles[1])), [HBM, VMEM]
         kernel = functools.partial(kernel, BACK, peers - 1)
         scratch = [pltpu.SMEM((1 + 2 * longest,), i32), pltpu.SemaphoreType.DMA((2,)), pltpu.SemaphoreType.DMA((places // LOAD,))]
     else:

time: 53.5 us -> 53.2 us (level); the launches traced: 53.9 us -> 53 us
  Pallas kernels: 39.5 us -> 37.7 us
  starting transfers between devices: 12.6 us -> 13.3 us
    pallas_call x1, Pallas kernels: 11.1 us -> 9.85 us  [shards(): pl.pallas_call(functools.partial(cross_kernel, width, keep), out_shape=(s...]
    all_to_all x1, starting transfers between devices: 5.33 us -> 5.95 us  [shards(): lax.all_to_all(payload2, AXES, split_axis=0, concat_axis=0, tiled=True)]
  transfers between devices with their start and end apart: 2 -> 2, of which waited for: 2 -> 2; matrix products, arithmetic and copies ran while one was open for 0% -> 0% of each run, Pallas kernels for 37% -> 38%
where the time goes in v1:
time: 53.2 us; the launch traced here: 53 us
  Pallas kernels  37.7 us (71%)
  starting transfers between devices  13.3 us (25%)
  waiting for transfers between devices  1.34 us (3%)
  between operations  0.68 us (1%)
    pallas_call x1, Pallas kernels, shards(): pl.pallas_call(functools.partial(local_kernel, width), out_shape=(shape((...  12.6 us
    pallas_call x1, Pallas kernels, shards(): pl.pallas_call(functools.partial(cross_kernel, width, keep), out_shape=(s...  9.85 us
    all_to_all x1, starting transfers between devices, shards(): lax.all_to_all(payload, AXES, split_axis=0, concat_axis=0, tiled=True)  7.3 us
    pallas_call x1, Pallas kernels, shards(): pl.pallas_call(functools.partial(back_local_kernel, BACK), out_shape=shap...  7.28 us
    all_to_all x1, starting transfers between devices, shards(): lax.all_to_all(payload2, AXES, split_axis=0, concat_axis=0, tiled=True)  5.95 us
    pallas_call x1, Pallas kernels, shards(): pl.pallas_call(kernel, out_shape=shape((flat_rows, HALF), f32), in_specs=...  5.84 us
    pallas_call x1, Pallas kernels, shards(): pl.pallas_call(pack_kernel, out_shape=(shape((peers, PEER_ROWS, HALF), i3...  2.13 us
  transfers between devices with their start and end apart: 2, of which 2 were waited for; matrix products, arithmetic and copies ran while one was open for 0% of the time, Pallas kernels for 38%

profile of v1, /device:TPU:0, one launch (start us, length us, event | category | flops | bytes accessed | tf_op | source)
XLA Modules:
  0.0 53.0 jit_solution(11943865143983318737)
XLA Ops:
  0.6 2.1 %pack.1 = (s32[32,24,128]{2,1,0:T(8,128)}, s32[64,8,128]{2,1,0:T(8,128)S(1)}) custom-call(s32[4,32]{1,0:T(4,128)} %bitcast.17, f32[3,16384]{1,0:T(4,128)} %cent_in.1, f32[128,128]{1,0:T(8,128)} %bitcast.12, f32[128,128]{1,0:T(8,128)} %bitcast.16), custom_call_target="tpu_custom_call" | custom-call | tf_op jit(solution)/shard_map/pack/pallas_call | solution.py:559
  2.8 7.3 %all-to-all-start = ((s32[32,24,128]{2,1,0:T(8,128)}), s32[32,24,128]{2,1,0:T(8,128)S(1)}, u32[]{:S(2)}, u32[]{:S(2)}) async-start(s32[32,24,128]{2,1,0:T(8,128)} %get-tuple-element.15), calls=%async_computation | async-start | bytes 786432 | tf_op jit(solution)/shard_map/all_to_all | solution.py:574
  10.1 12.6 %local.1 = (f32[64,8,256]{2,1,0:T(8,128)S(1)}, bf16[128,256,256]{2,1,0:T(8,128)(2,1)}, bf16[64,32,256]{2,1,0:T(8,128)(2,1)S(1)}, s32[513]{0:T(1024)S(1)}) custom-call(s32[64]{0:T(128)} %first_in.3, s32[64]{0:T(128)} %second_in.3, s32[1,32]{1,0:T(1,128)} %counts_in.1, s32[4,32]{1,0:T(4,128)} %bitcast.18, s32[64,8,128]{2,1,0:T(8,128)S(1)} %get-tuple-element.13.words), custom_call_target="tpu_custom_call" | custom-call | flops 838860800 | bytes 1048576 | tf_op jit(solution)/shard_map/local/pallas_call | solution.py:575
  22.7 0.9 %all-to-all-done = s32[32,24,128]{2,1,0:T(8,128)S(1)} async-done(((s32[32,24,128]{2,1,0:T(8,128)}), s32[32,24,128]{2,1,0:T(8,128)S(1)}, u32[]{:S(2)}, u32[]{:S(2)}) %all-to-all-start) | async-done | bytes 393248 | tf_op jit(solution)/shard_map/all_to_all | solution.py:574
  23.6 9.9 %cross.1 = (f32[128,128]{1,0:T(8,128)}, f32[128,128]{1,0:T(8,128)S(1)}, f32[32,8,128]{2,1,0:T(8,128)}, bf16[128,256,256]{2,1,0:T(8,128)(2,1)}, bf16[8,256,256]{2,1,0:T(8,128)(2,1)S(1)}) custom-call(s32[513]{0:T(1024)S(1)} %get-tuple-element.14.plan.plan_in, s32[4,32]{1,0:T(4,128)} %bitcast.19, s32[768,128]{1,0:T(8,128)S(1)} %bitcast.10, ...), custom_call_target="tpu_custom_call" | custom-call | tf_op jit(solution)/shard_map/cross/pallas_call | solution.py:607
  33.5 5.9 %all-to-all-start.1 = ((f32[32,8,128]{2,1,0:T(8,128)}), f32[32,8,128]{2,1,0:T(8,128)S(1)}, u32[]{:S(2)}, u32[]{:S(2)}) async-start(f32[32,8,128]{2,1,0:T(8,128)} %get-tuple-element.19), calls=%async_computation.1 | async-start | bytes 262144 | tf_op jit(solution)/shard_map/all_to_all | solution.py:631
  39.4 7.3 %back_local.1.total_in = f32[64,8,256]{2,1,0:T(8,128)S(1)} custom-call(s32[64]{0:T(128)} %first_in.3, s32[64]{0:T(128)} %second_in.3, f32[128,128]{1,0:T(8,128)S(1)} %get-tuple-element.22.ratio, bf16[128,256,256]{2,1,0:T(8,128)(2,1)} %get-tuple-element.23.kept), custom_call_target="tpu_custom_call" | custom-call | flops 838860800 | bytes 1048576 | tf_op jit(solution)/shard_map/back_local/pallas_call | solution.py:632
  46.7 0.5 all-to-all-done.1
  47.2 5.8 %back_cross.1 = f32[128,128]{1,0:T(8,128)} custom-call(s32[513]{0:T(1024)S(1)} %get-tuple-element.14.plan.plan_in, f32[256,128]{1,0:T(8,128)S(1)} %bitcast.11, bf16[128,256,256]{2,1,0:T(8,128)(2,1)} %get-tuple-element.20.kept, bf16[8,256,256]{2,1,0:T(8,128)(2,1)S(1)} %get-tuple-element.21.stay, f32[64,8,256]{2,1,0:T(8,128)S(1)} %back_local.1.total_in, ...), custom_call_target="tpu_custom_call" | custom-call | tf_op jit(solution)/shard_map/back_cross/pallas_call | solution.py:660
Async XLA Ops:
  2.8 20.9 %all-to-all-start = ((s32[32,24,128]{2,1,0:T(8,128)}), s32[32,24,128]{2,1,0:T(8,128)S(1)}, u32[]{:S(2)}, u32[]{:S(2)}) async-start(s32[32,24,128]{2,1,0:T(8,128)} %get-tuple-element.15), calls=%async_computation | async-start | bytes 786432 | tf_op jit(solution)/shard_map/all_to_all | solution.py:574
  33.5 13.7 %all-to-all-start.1 = ((f32[32,8,128]{2,1,0:T(8,128)}), f32[32,8,128]{2,1,0:T(8,128)S(1)}, u32[]{:S(2)}, u32[]{:S(2)}) async-start(f32[32,8,128]{2,1,0:T(8,128)} %get-tuple-element.19), calls=%async_computation.1 | async-start | bytes 262144 | tf_op jit(solution)/shard_map/all_to_all | solution.py:631

commit v2 on v0

--- a/solution.py
+++ b/solution.py
@@ -321,7 +321,7 @@
     kept = None
     if keep:
         kept, *rest = rest
-    ring, total, flat, vals, sens, chosen, squares, sums0, sems, *ring_sems = rest
+    ring, total, flat, vals, sens, chosen, squares, sums0, sends, filts, sems, out_sems, *ring_sems = rest
     blocks = near.shape[0]
     waits = fetch([(chosen_in, chosen), (sens_in, sens)], sems)
     total[...] = total_in[...]
@@ -351,26 +351,32 @@
     for wait in waits:
         wait()
     base = total[:, 3, :]
+    for half in range(2):
+        rows = pl.ds(half, blocks, stride=2)
+        part = sens[rows, :] / base[:, half * HALF : (half + 1) * HALF]
+        flat[rows, :] = part.astype(jnp.bfloat16).astype(jnp.float32)
+
+    def send(p, carry):
+        for s in range(slots):
+            sends[p, 2 * s : 2 * s + 2, :] = flat[pl.ds(2 * chosen[s, p], 2), :]
+        return carry
+
+    lax.fori_loop(0, peers, send, 0, unroll=4)
+    sent = pltpu.make_async_copy(sends, payload, out_sems.at[0])
+    sent.start()
     filt = total[:, 4, :] / base
+    ratio[...] = jnp.zeros_like(ratio)
     for half in range(2):
         rows = pl.ds(half, blocks, stride=2)
         lanes = slice(half * HALF, (half + 1) * HALF)
-        filtered[rows, :] = filt[:, lanes]
-        part = sens[rows, :] / base[:, lanes]
-        flat[rows, :] = part.astype(jnp.bfloat16).astype(jnp.float32)
-    ratio[...] = jnp.zeros_like(ratio)
-    for half in range(2):
-        lanes = slice(half * HALF, (half + 1) * HALF)
-        ratio[:, 0, lanes] = flat[pl.ds(half, blocks, stride=2), :]
-
-    def send(p, carry):
-        for s in range(slots):
-            payload[p, 2 * s : 2 * s + 2, :] = flat[pl.ds(2 * chosen[s, p], 2), :]
-        return carry
-
-    lax.fori_loop(0, peers, send, 0, unroll=4)
+        filts[rows, :] = filt[:, lanes]
+        ratio[:, 0, lanes] = flat[rows, :]
+    written = pltpu.make_async_copy(filts, filtered, out_sems.at[1])
+    written.start()
     if keep:
         wait_tiles()
+    sent.wait()
+    written.wait()
 
 
 def tile_loads(width, kept, tiles, sems):
@@ -599,13 +605,13 @@
     filtered, ratio, payload2, *cross_tiles = pl.pallas_call(
         functools.partial(cross_kernel, width, keep),
         out_shape=(
-            shape((flat_rows, HALF), f32),
+            pltpu.HBM((flat_rows, HALF), f32),
             shape((blocks, ROWS, BLK), f32),
-            shape((peers, 2 * slots, HALF), f32),
+            pltpu.HBM((peers, 2 * slots, HALF), f32),
         )
         + ((pltpu.HBM((held, BLK, BLK), bf16),) if keep else ()),
         in_specs=[SMEM, HBM, VMEM, VMEM, VMEM, HBM],
-        out_specs=(VMEM, VMEM, VMEM) + ((HBM,) if keep else ()),
+        out_specs=(HBM, VMEM, HBM) + ((HBM,) if keep else ()),
         scratch_shapes=[
             ring,
             sums,
@@ -615,6 +621,9 @@
             table,
             square,
             results,
+            pltpu.VMEM((peers, 2 * slots, HALF), f32),
+            flat,
+            pltpu.SemaphoreType.DMA((2,)),
             pltpu.SemaphoreType.DMA((2,)),
         ]
         + ([ring_sems] if keep else []),

time: 53.5 us -> 53.6 us (level); the launches traced: 53.9 us -> 52.7 us
  Pallas kernels: 39.5 us -> 37.3 us
  starting transfers between devices: 12.6 us -> 13.7 us
    pallas_call x1, Pallas kernels: 11.1 us -> 9.46 us  [shards(): pl.pallas_call(functools.partial(cross_kernel, width, keep), out_shape=(p...]
    all_to_all x1, starting transfers between devices: 5.33 us -> 6.37 us  [shards(): lax.all_to_all(payload2, AXES, split_axis=0, concat_axis=0, tiled=True)]
    pallas_call x1, Pallas kernels: 6.13 us -> 5.53 us  [shards(): pl.pallas_call(kernel, out_shape=shape((flat_rows, HALF), f32), in_specs=...]
  transfers between devices with their start and end apart: 2 -> 2, of which waited for: 2 -> 2; matrix products, arithmetic and copies ran while one was open for 0% -> 0% of each run, Pallas kernels for 37% -> 38%
where the time goes in v2:
time: 53.6 us; the launch traced here: 52.7 us
  Pallas kernels  37.3 us (70%)
  starting transfers between devices  13.7 us (26%)
  waiting for transfers between devices  1.08 us (2%)
  between operations  0.68 us (1%)
    pallas_call x1, Pallas kernels, shards(): pl.pallas_call(functools.partial(local_kernel, width), out_shape=(shape((...  12.9 us
    pallas_call x1, Pallas kernels, shards(): pl.pallas_call(functools.partial(cross_kernel, width, keep), out_shape=(p...  9.46 us
    all_to_all x1, starting transfers between devices, shards(): lax.all_to_all(payload, AXES, split_axis=0, concat_axis=0, tiled=True)  7.3 us
    pallas_call x1, Pallas kernels, shards(): pl.pallas_call(functools.partial(back_local_kernel, BACK), out_shape=shap...  7.26 us
    all_to_all x1, starting transfers between devices, shards(): lax.all_to_all(payload2, AXES, split_axis=0, concat_axis=0, tiled=True)  6.37 us
    pallas_call x1, Pallas kernels, shards(): pl.pallas_call(kernel, out_shape=shape((flat_rows, HALF), f32), in_specs=...  5.53 us
    pallas_call x1, Pallas kernels, shards(): pl.pallas_call(pack_kernel, out_shape=(shape((peers, PEER_ROWS, HALF), i3...  2.13 us
  transfers between devices with their start and end apart: 2, of which 2 were waited for; matrix products, arithmetic and copies ran while one was open for 0% of the time, Pallas kernels for 38%

profile of v2, /device:TPU:0, one launch (start us, length us, event | category | flops | bytes accessed | tf_op | source)
XLA Modules:
  0.0 52.7 jit_solution(5827604181501804744)
XLA Ops:
  0.6 2.1 %pack.1 = (s32[32,24,128]{2,1,0:T(8,128)}, s32[64,8,128]{2,1,0:T(8,128)S(1)}) custom-call(s32[4,32]{1,0:T(4,128)} %bitcast.17, f32[3,16384]{1,0:T(4,128)} %cent_in.1, f32[128,128]{1,0:T(8,128)} %bitcast.12, f32[128,128]{1,0:T(8,128)} %bitcast.16), custom_call_target="tpu_custom_call" | custom-call | tf_op jit(solution)/shard_map/pack/pallas_call | solution.py:557
  2.8 7.3 %all-to-all-start = ((s32[32,24,128]{2,1,0:T(8,128)}), s32[32,24,128]{2,1,0:T(8,128)S(1)}, u32[]{:S(2)}, u32[]{:S(2)}) async-start(s32[32,24,128]{2,1,0:T(8,128)} %get-tuple-element.14), calls=%async_computation | async-start | bytes 786432 | tf_op jit(solution)/shard_map/all_to_all | solution.py:572
  10.1 12.9 %local.1 = (f32[64,8,256]{2,1,0:T(8,128)S(1)}, bf16[128,256,256]{2,1,0:T(8,128)(2,1)}, bf16[64,32,256]{2,1,0:T(8,128)(2,1)S(1)}, s32[513]{0:T(1024)S(1)}) custom-call(s32[64]{0:T(128)} %first_in.3, s32[64]{0:T(128)} %second_in.3, s32[1,32]{1,0:T(1,128)} %counts_in.1, s32[4,32]{1,0:T(4,128)} %bitcast.18, s32[64,8,128]{2,1,0:T(8,128)S(1)} %get-tuple-element.12.words), custom_call_target="tpu_custom_call" | custom-call | flops 838860800 | bytes 1048576 | tf_op jit(solution)/shard_map/local/pallas_call | solution.py:573
  23.0 0.6 %all-to-all-done = s32[32,24,128]{2,1,0:T(8,128)S(1)} async-done(((s32[32,24,128]{2,1,0:T(8,128)}), s32[32,24,128]{2,1,0:T(8,128)S(1)}, u32[]{:S(2)}, u32[]{:S(2)}) %all-to-all-start) | async-done | bytes 393248 | tf_op jit(solution)/shard_map/all_to_all | solution.py:572
  23.6 9.5 %cross.1 = (f32[128,128]{1,0:T(8,128)}, f32[64,8,256]{2,1,0:T(8,128)S(1)}, f32[32,8,128]{2,1,0:T(8,128)}, bf16[128,256,256]{2,1,0:T(8,128)(2,1)}) custom-call(s32[513]{0:T(1024)S(1)} %get-tuple-element.13.plan.plan_in, s32[4,32]{1,0:T(4,128)} %bitcast.19, s32[768,128]{1,0:T(8,128)S(1)} %bitcast.10, bf16[64,32,256]{2,1,0:T(8,128)(2,1)S(1)} %get-tuple-element.15.near, ...), custom_call_target="tpu_custom_call" | custom-call | tf_op jit(solution)/shard_map/cross/pallas_call | solution.py:605
  33.1 6.4 %all-to-all-start.1 = ((f32[32,8,128]{2,1,0:T(8,128)}), f32[32,8,128]{2,1,0:T(8,128)S(1)}, u32[]{:S(2)}, u32[]{:S(2)}) async-start(f32[32,8,128]{2,1,0:T(8,128)} %get-tuple-element.18), calls=%async_computation.1 | async-start | bytes 262144 | tf_op jit(solution)/shard_map/all_to_all | solution.py:633
  39.5 7.3 %back_local.1.total_in = f32[64,8,256]{2,1,0:T(8,128)S(1)} custom-call(s32[64]{0:T(128)} %first_in.3, s32[64]{0:T(128)} %second_in.3, f32[64,8,256]{2,1,0:T(8,128)S(1)} %get-tuple-element.20.ratio, bf16[128,256,256]{2,1,0:T(8,128)(2,1)} %get-tuple-element.21.kept), custom_call_target="tpu_custom_call" | custom-call | flops 838860800 | bytes 1048576 | tf_op jit(solution)/shard_map/back_local/pallas_call | solution.py:634
  46.7 0.5 all-to-all-done.1
  47.2 5.5 %back_cross.1 = f32[128,128]{1,0:T(8,128)} custom-call(s32[513]{0:T(1024)S(1)} %get-tuple-element.13.plan.plan_in, f32[256,128]{1,0:T(8,128)S(1)} %bitcast.11, bf16[128,256,256]{2,1,0:T(8,128)(2,1)} %get-tuple-element.19.kept, f32[64,8,256]{2,1,0:T(8,128)S(1)} %back_local.1.total_in, f32[128,128]{1,0:T(8,128)} %bitcast.13), custom_call_target="tpu_custom_call" | custom-call | tf_op jit(solution)/shard_map/back_cross/pallas_call | solution.py:662
Async XLA Ops:
  2.8 20.9 %all-to-all-start = ((s32[32,24,128]{2,1,0:T(8,128)}), s32[32,24,128]{2,1,0:T(8,128)S(1)}, u32[]{:S(2)}, u32[]{:S(2)}) async-start(s32[32,24,128]{2,1,0:T(8,128)} %get-tuple-element.14), calls=%async_computation | async-start | bytes 786432 | tf_op jit(solution)/shard_map/all_to_all | solution.py:572
  33.1 14.1 %all-to-all-start.1 = ((f32[32,8,128]{2,1,0:T(8,128)}), f32[32,8,128]{2,1,0:T(8,128)S(1)}, u32[]{:S(2)}, u32[]{:S(2)}) async-start(f32[32,8,128]{2,1,0:T(8,128)} %get-tuple-element.18), calls=%async_computation.1 | async-start | bytes 262144 | tf_op jit(solution)/shard_map/all_to_all | solution.py:633

commit v3 on v2

--- a/solution.py
+++ b/solution.py
@@ -40,7 +40,7 @@
     return first | (second << 16)
 
 
-def pack_kernel(chosen_in, cent_in, vol_in, dens_in, payload, words, chosen, cent, vol, dens, sems):
+def pack_kernel(chosen_in, cent_in, vol_in, dens_in, payload, words, chosen, cent, vol, dens, sends, sems, out_sems):
     blocks = words.shape[0]
     waits = fetch(
         [(cent_in, cent), (vol_in, vol), (dens_in, dens), (chosen_in, chosen)], sems
@@ -60,10 +60,19 @@
 
     def send(p, carry):
         for s in range(slots):
-            payload[p, WORDS * s : WORDS * (s + 1), :] = words[chosen[s, p], 0:WORDS, :]
+            sends[p, WORDS * s : WORDS * (s + 1), :] = words[chosen[s, p], 0:WORDS, :]
         return carry
 
-    lax.fori_loop(0, peers, send, 0, unroll=4)
+    chunks = out_sems.shape[0]
+    share = peers // chunks
+    copies = []
+    for c in range(chunks):
+        lax.fori_loop(c * share, (c + 1) * share, send, 0, unroll=4)
+        part = pl.ds(c * share, share)
+        copies.append(pltpu.make_async_copy(sends.at[part], payload.at[part], out_sems.at[c]))
+        copies[-1].start()
+    for copy in copies:
+        copy.wait()
 
 
 def decode(word):
@@ -556,14 +565,16 @@
 
     payload, words = pl.pallas_call(
         pack_kernel,
-        out_shape=(shape((peers, PEER_ROWS, HALF), i32), shape((blocks, ROWS, HALF), i32)),
+        out_shape=(pltpu.HBM((peers, PEER_ROWS, HALF), i32), shape((blocks, ROWS, HALF), i32)),
         in_specs=[HBM] * 4,
-        out_specs=(VMEM, VMEM),
+        out_specs=(HBM, VMEM),
         scratch_shapes=[
             table,
             pltpu.VMEM(centroids.shape, f32),
             flat,
             flat,
+            pltpu.VMEM((peers, PEER_ROWS, HALF), i32),
+            pltpu.SemaphoreType.DMA((4,)),
             pltpu.SemaphoreType.DMA((4,)),
         ],
         compiler_params=params(8),

time: 53.6 us -> 52.3 us (0.976)
  the two profiles are of different devices: /device:TPU:0 before, /device:TPU:1 now
where the time goes in v3:
time: 52.3 us; the launch traced here: 51.8 us
  Pallas kernels  37.8 us (72%)
  starting transfers between devices  12.9 us (25%)
  between operations  0.68 us (1%)
    pallas_call x1, Pallas kernels, shards(): pl.pallas_call(functools.partial(local_kernel, width), out_shape=(shape((...  12.9 us
    pallas_call x1, Pallas kernels, shards(): pl.pallas_call(functools.partial(cross_kernel, width, keep), out_shape=(p...  9.46 us
    pallas_call x1, Pallas kernels, shards(): pl.pallas_call(functools.partial(back_local_kernel, BACK), out_shape=shap...  7.26 us
    all_to_all x1, starting transfers between devices, shards(): lax.all_to_all(payload, AXES, split_axis=0, concat_axis=0, tiled=True)  7.1 us
    pallas_call x1, Pallas kernels, shards(): pl.pallas_call(kernel, out_shape=shape((flat_rows, HALF), f32), in_specs=...  6.13 us
    all_to_all x1, starting transfers between devices, shards(): lax.all_to_all(payload2, AXES, split_axis=0, concat_axis=0, tiled=True)  5.8 us
    pallas_call x1, Pallas kernels, shards(): pl.pallas_call(pack_kernel, out_shape=(pltpu.HBM((peers, PEER_ROWS, HALF)...  2.04 us
  transfers between devices with their start and end apart: 2, of which 1 were waited for; matrix products, arithmetic and copies ran while one was open for 0% of the time, Pallas kernels for 39%

profile of v3, /device:TPU:1, one launch (start us, length us, event | category | flops | bytes accessed | tf_op | source)
XLA Modules:
  0.0 51.8 jit_solution(13742885030270166145)
XLA Ops:
  0.6 2.0 %pack.1 = (s32[32,24,128]{2,1,0:T(8,128)}, s32[64,8,128]{2,1,0:T(8,128)S(1)}) custom-call(s32[4,32]{1,0:T(4,128)} %bitcast.17, f32[3,16384]{1,0:T(4,128)} %cent_in.1, f32[128,128]{1,0:T(8,128)} %bitcast.12, f32[128,128]{1,0:T(8,128)} %bitcast.16), custom_call_target="tpu_custom_call" | custom-call | tf_op jit(solution)/shard_map/pack/pallas_call | solution.py:566
  2.7 7.1 %all-to-all-start = ((s32[32,24,128]{2,1,0:T(8,128)}), s32[32,24,128]{2,1,0:T(8,128)S(1)}, u32[]{:S(2)}, u32[]{:S(2)}) async-start(s32[32,24,128]{2,1,0:T(8,128)} %get-tuple-element.14), calls=%async_computation | async-start | bytes 786432 | tf_op jit(solution)/shard_map/all_to_all | solution.py:583
  9.8 12.9 %local.1 = (f32[64,8,256]{2,1,0:T(8,128)S(1)}, bf16[128,256,256]{2,1,0:T(8,128)(2,1)}, bf16[64,32,256]{2,1,0:T(8,128)(2,1)S(1)}, s32[513]{0:T(1024)S(1)}) custom-call(s32[64]{0:T(128)} %first_in.3, s32[64]{0:T(128)} %second_in.3, s32[1,32]{1,0:T(1,128)} %counts_in.1, s32[4,32]{1,0:T(4,128)} %bitcast.18, s32[64,8,128]{2,1,0:T(8,128)S(1)} %get-tuple-element.12.words), custom_call_target="tpu_custom_call" | custom-call | flops 838860800 | bytes 1048576 | tf_op jit(solution)/shard_map/local/pallas_call | solution.py:584
  22.7 0.0 all-to-all-done
  22.8 9.5 %cross.1 = (f32[128,128]{1,0:T(8,128)}, f32[64,8,256]{2,1,0:T(8,128)S(1)}, f32[32,8,128]{2,1,0:T(8,128)}, bf16[128,256,256]{2,1,0:T(8,128)(2,1)}) custom-call(s32[513]{0:T(1024)S(1)} %get-tuple-element.13.plan.plan_in, s32[4,32]{1,0:T(4,128)} %bitcast.19, s32[768,128]{1,0:T(8,128)S(1)} %bitcast.10, bf16[64,32,256]{2,1,0:T(8,128)(2,1)S(1)} %get-tuple-element.15.near, ...), custom_call_target="tpu_custom_call" | custom-call | tf_op jit(solution)/shard_map/cross/pallas_call | solution.py:616
  32.2 5.8 %all-to-all-start.1 = ((f32[32,8,128]{2,1,0:T(8,128)}), f32[32,8,128]{2,1,0:T(8,128)S(1)}, u32[]{:S(2)}, u32[]{:S(2)}) async-start(f32[32,8,128]{2,1,0:T(8,128)} %get-tuple-element.18), calls=%async_computation.1 | async-start | bytes 262144 | tf_op jit(solution)/shard_map/all_to_all | solution.py:644
  38.0 7.3 %back_local.1.total_in = f32[64,8,256]{2,1,0:T(8,128)S(1)} custom-call(s32[64]{0:T(128)} %first_in.3, s32[64]{0:T(128)} %second_in.3, f32[64,8,256]{2,1,0:T(8,128)S(1)} %get-tuple-element.20.ratio, bf16[128,256,256]{2,1,0:T(8,128)(2,1)} %get-tuple-element.21.kept), custom_call_target="tpu_custom_call" | custom-call | flops 838860800 | bytes 1048576 | tf_op jit(solution)/shard_map/back_local/pallas_call | solution.py:645
  45.3 0.3 all-to-all-done.1
  45.6 6.1 %back_cross.1 = f32[128,128]{1,0:T(8,128)} custom-call(s32[513]{0:T(1024)S(1)} %get-tuple-element.13.plan.plan_in, f32[256,128]{1,0:T(8,128)S(1)} %bitcast.11, bf16[128,256,256]{2,1,0:T(8,128)(2,1)} %get-tuple-element.19.kept, f32[64,8,256]{2,1,0:T(8,128)S(1)} %back_local.1.total_in, f32[128,128]{1,0:T(8,128)} %bitcast.13), custom_call_target="tpu_custom_call" | custom-call | tf_op jit(solution)/shard_map/back_cross/pallas_call | solution.py:673
Async XLA Ops:
  2.7 20.1 %all-to-all-start = ((s32[32,24,128]{2,1,0:T(8,128)}), s32[32,24,128]{2,1,0:T(8,128)S(1)}, u32[]{:S(2)}, u32[]{:S(2)}) async-start(s32[32,24,128]{2,1,0:T(8,128)} %get-tuple-element.14), calls=%async_computation | async-start | bytes 786432 | tf_op jit(solution)/shard_map/all_to_all | solution.py:583
  32.2 13.4 %all-to-all-start.1 = ((f32[32,8,128]{2,1,0:T(8,128)}), f32[32,8,128]{2,1,0:T(8,128)S(1)}, u32[]{:S(2)}, u32[]{:S(2)}) async-start(f32[32,8,128]{2,1,0:T(8,128)} %get-tuple-element.18), calls=%async_computation.1 | async-start | bytes 262144 | tf_op jit(solution)/shard_map/all_to_all | solution.py:644
